TPU v7x, 32 devices: a whole 2x2x4 slice. The times are simulated.
32 devices in a mesh: fsdp: 32 (over z, y, x, core).
Axes of the slice: x: 2, y: 2, z: 4, core: 2. Of those that a mesh axis runs over, the one named last changes fastest.
Arguments:
- tokens: bfloat16 [65536, 768], P('fsdp'), may hold values from -6 to 6
- cotangent: bfloat16 [65536, 768], P('fsdp'), may hold values from -6 to 6
- segments: int32 [65536], P('fsdp'), may hold values from 0 to 1, as said below
- positions: int32 [65536], P('fsdp'), may hold values from 0 to 1999, as said below
- qkv_weight: float32 [768, 2304], P('fsdp'), may hold values from -0.21875 to 0.21875
- qkv_first: float32 [768, 2304], P('fsdp'), may hold values from -160 to 160
- qkv_second: float32 [768, 2304], P('fsdp'), may hold values from 1310 to 5461
- out_weight: float32 [768, 768], P('fsdp'), may hold values from -0.625 to 0.625
- out_first: float32 [768, 768], P('fsdp'), may hold values from -160 to 160
- out_second: float32 [768, 768], P('fsdp'), may hold values from 1310 to 5461
- in_weight: float32 [768, 2304], P('fsdp'), may hold values from -0.21875 to 0.21875
- in_first: float32 [768, 2304], P('fsdp'), may hold values from -160 to 160
- in_second: float32 [768, 2304], P('fsdp'), may hold values from 1310 to 5461
- down_weight: float32 [1152, 768], P('fsdp'), may hold values from -0.375 to 0.375
- down_first: float32 [1152, 768], P('fsdp'), may hold values from -160 to 160
- down_second: float32 [1152, 768], P('fsdp'), may hold values from 1310 to 5461
- norm_gains: float32 [2, 768], P(None, 'fsdp'), may hold values from 0.5 to 1.5
- gains_first: float32 [2, 768], P(None, 'fsdp'), may hold values from -160 to 160
- gains_second: float32 [2, 768], P(None, 'fsdp'), may hold values from 1310 to 5461
Outputs:
- activations: bfloat16 [65536, 768], P('fsdp')
- input_grad: float32 [65536, 768], P('fsdp')
- qkv_grad: float32 [768, 2304], P('fsdp')
- qkv_new: float32 [768, 2304], P('fsdp')
- qkv_first_new: float32 [768, 2304], P('fsdp')
- qkv_second_new: float32 [768, 2304], P('fsdp')
- out_grad: float32 [768, 768], P('fsdp')
- out_new: float32 [768, 768], P('fsdp')
- out_first_new: float32 [768, 768], P('fsdp')
- out_second_new: float32 [768, 768], P('fsdp')
- in_grad: float32 [768, 2304], P('fsdp')
- in_new: float32 [768, 2304], P('fsdp')
- in_first_new: float32 [768, 2304], P('fsdp')
- in_second_new: float32 [768, 2304], P('fsdp')
- down_grad: float32 [1152, 768], P('fsdp')
- down_new: float32 [1152, 768], P('fsdp')
- down_first_new: float32 [1152, 768], P('fsdp')
- down_second_new: float32 [1152, 768], P('fsdp')
- gains_grad: float32 [2, 768], P(None, 'fsdp')
- gains_delta: float32 [2, 768], P(None, 'fsdp')
- gains_first_new: float32 [2, 768], P(None, 'fsdp')
- gains_second_new: float32 [2, 768], P(None, 'fsdp')
Inputs may be any that keep to these rules, and one draw needn't show every extreme that they name: `segments`: documents lie end to end over all 65536 tokens; the segment number is 0 on the first document and changes between 0 and 1 from each document to the next. Each document is 200 to 2000 tokens long, the last cut at the end, and both lengths occur. A document may run across packed sequences. `positions`: place of each token in its document counted from 0; it grows by one from token to token inside a document and starts again at 0 where the segment number changes.
All inputs are finite; a program needn't handle non-finite values.
Results may differ from a plain program's by a relative error of at most 0.019.
Values may be sent and summed in bfloat16 or wider, within the bound.
A program may use at most 256 MiB of HBM per device.

v0:
```python
import jax
import jax.numpy as jnp
from jax import lax
from jax.sharding import PartitionSpec as P

D = 768
HEADS = 12
HEAD = 64
FF = 1152
SEQ = 512
BLK = 128
STEP = 10


NORM_EPS = 1e-05
BETA_ONE = 0.9
BETA_TWO = 0.98
ADAM_EPS = 1e-06
LEARN_RATE = 0.1
WEIGHT_DECAY = 0.01
ROPE_BASE = 10000.0
MASKED = -1e30


def layer_norm(values, norm_gain):
    center = values - jnp.mean(values, axis=-1, keepdims=True)
    spread = jnp.mean(center * center, axis=-1, keepdims=True)
    return center * lax.rsqrt(spread + NORM_EPS) * norm_gain


def rotate(values, cosine, sine):
    half_dim = values.shape[-1] // 2
    turned = jnp.concatenate([-values[..., half_dim:], values[..., :half_dim]], axis=-1)
    return values * cosine + turned * sine


def rope_tables(places):
    half_dim = HEAD // 2
    frequency = ROPE_BASE ** (-(jnp.arange(half_dim).astype(jnp.float32) * 2.0 / HEAD))
    angles = places.astype(jnp.float32)[:, None] * frequency[None, :]
    angles = jnp.concatenate([angles, angles], axis=-1)
    return (jnp.cos(angles)[:, None, :], jnp.sin(angles)[:, None, :])


def widen(blocked):
    before = jnp.roll(blocked, 1, axis=0)
    after = jnp.roll(blocked, -1, axis=0)
    return jnp.concatenate([before, blocked, after], axis=1)


def fold_wide(wide):
    block_width = wide.shape[1] // 3
    middle = wide[:, block_width : 2 * block_width]
    return (
        middle
        + jnp.roll(wide[:, :block_width], -1, axis=0)
        + jnp.roll(wide[:, 2 * block_width :], 1, axis=0)
    )


def window_mask(seq_segs, block_width):
    row_count = seq_segs.shape[0]
    block_count = row_count // block_width
    starts = jnp.arange(block_count)[:, None, None] * block_width
    query_at = starts + jnp.arange(block_width)[None, :, None]
    key_at = starts - block_width + jnp.arange(3 * block_width)[None, None, :]
    seg_blocks = seq_segs.reshape(block_count, block_width)
    seg_wide = widen(seg_blocks)
    in_window = jnp.abs(query_at - key_at) <= block_width // 2
    inside = (key_at >= 0) & (key_at < row_count)
    same_doc = seg_blocks[:, :, None] == seg_wide[:, None, :]
    return in_window & inside & same_doc


def block_scores(query_heads, key_heads, seq_segs):
    block_count = query_heads.shape[0] // BLK
    query_blocks = query_heads.reshape(block_count, BLK, HEADS, HEAD)
    key_wide = widen(key_heads.reshape(block_count, BLK, HEADS, HEAD))
    scores = jnp.einsum(
        "bqhe,bkhe->bhqk", query_blocks, key_wide, preferred_element_type=jnp.float32
    ) * HEAD ** (-0.5)
    allowed = window_mask(seq_segs, BLK)[:, None]
    return (jnp.where(allowed, scores, MASKED), query_blocks, key_wide)


def attend(seq_items):
    query_heads, key_heads, value_heads, seq_segs = seq_items
    scores, query_blocks, key_wide = block_scores(query_heads, key_heads, seq_segs)
    row_top = jnp.max(scores, axis=-1, keepdims=True)
    exp_scores = jnp.exp(scores - row_top)
    row_total = jnp.sum(exp_scores, axis=-1, keepdims=True)
    prob_low = (exp_scores / row_total).astype(jnp.bfloat16)
    value_wide = widen(value_heads.reshape(query_blocks.shape))
    attended = jnp.einsum(
        "bhqk,bkhe->bqhe", prob_low, value_wide, preferred_element_type=jnp.float32
    )
    return (attended.reshape(value_heads.shape).astype(jnp.bfloat16), row_top + jnp.log(row_total))


def attend_back(seq_items):
    query_heads, key_heads, value_heads, grad_heads, log_total, seq_segs = seq_items
    scores, query_blocks, key_wide = block_scores(query_heads, key_heads, seq_segs)
    value_wide = widen(value_heads.reshape(query_blocks.shape))
    grad_blocks = grad_heads.reshape(query_blocks.shape)
    attn_prob = jnp.exp(scores - log_total)
    prob_low = attn_prob.astype(jnp.bfloat16)
    grad_value_wide = jnp.einsum(
        "bhqk,bqhe->bkhe", prob_low, grad_blocks, preferred_element_type=jnp.float32
    )
    grad_prob = jnp.einsum(
        "bqhe,bkhe->bhqk", grad_blocks, value_wide, preferred_element_type=jnp.float32
    )
    inner = jnp.sum(attn_prob * grad_prob, axis=-1, keepdims=True)
    grad_scores = (attn_prob * (grad_prob - inner)).astype(jnp.bfloat16)
    scale_factor = HEAD ** (-0.5)
    grad_query = (
        jnp.einsum("bhqk,bkhe->bqhe", grad_scores, key_wide, preferred_element_type=jnp.float32)
        * scale_factor
    )
    grad_key_wide = (
        jnp.einsum("bhqk,bqhe->bkhe", grad_scores, query_blocks, preferred_element_type=jnp.float32)
        * scale_factor
    )
    head_shape = query_heads.shape
    return (
        grad_query.reshape(head_shape),
        fold_wide(grad_key_wide).reshape(head_shape),
        fold_wide(grad_value_wide).reshape(head_shape),
    )


def split_seqs(array, seq_count):
    return array.reshape((seq_count, SEQ) + array.shape[1:])


def adam_step(master, weight_grad, moment_one, moment_two):
    first_new = BETA_ONE * moment_one + (1.0 - BETA_ONE) * weight_grad
    second_new = BETA_TWO * moment_two + (1.0 - BETA_TWO) * weight_grad * weight_grad
    first_hat = first_new / (1.0 - BETA_ONE**STEP)
    second_hat = second_new / (1.0 - BETA_TWO**STEP)
    master_new = master - LEARN_RATE * (
        first_hat / (jnp.sqrt(second_hat) + ADAM_EPS) + WEIGHT_DECAY * master
    )
    return (weight_grad, master_new, first_new, second_new)


def geglu(gate_up):
    return jax.nn.gelu(gate_up[:, :FF], approximate=False) * gate_up[:, FF:]


def shards(
    tokens,
    cotangent,
    segments,
    positions,
    qkv_weight,
    qkv_first,
    qkv_second,
    out_weight,
    out_first,
    out_second,
    in_weight,
    in_first,
    in_second,
    down_weight,
    down_first,
    down_second,
    norm_gains,
    gains_first,
    gains_second,
):
    masters = (qkv_weight, out_weight, in_weight, down_weight, norm_gains)
    rounded = tuple((master.astype(jnp.bfloat16) for master in masters))
    gathered = (
        lax.all_gather(rounded[0], "fsdp", axis=0, tiled=True),
        lax.all_gather(rounded[1], "fsdp", axis=0, tiled=True),
        lax.all_gather(rounded[2], "fsdp", axis=0, tiled=True),
        lax.all_gather(rounded[3], "fsdp", axis=0, tiled=True),
        lax.all_gather(rounded[4], "fsdp", axis=1, tiled=True),
    )
    qkv_low, out_low, in_low, down_low, gains_low = gathered
    gains_full = gains_low.astype(jnp.float32)
    row_count = tokens.shape[0]
    seq_count = row_count // SEQ
    hidden_in = tokens.astype(jnp.float32)
    normed, norm_back_one = jax.vjp(layer_norm, hidden_in, gains_full[0])
    normed_low = normed.astype(jnp.bfloat16)
    qkv_mixed = jnp.dot(normed_low, qkv_low, preferred_element_type=jnp.float32)
    cosine, sine = rope_tables(positions)
    query_heads = rotate(qkv_mixed[:, :D].reshape(row_count, HEADS, HEAD), cosine, sine).astype(
        jnp.bfloat16
    )
    key_heads = rotate(
        qkv_mixed[:, D : 2 * D].reshape(row_count, HEADS, HEAD), cosine, sine
    ).astype(jnp.bfloat16)
    value_heads = qkv_mixed[:, 2 * D :].reshape(row_count, HEADS, HEAD).astype(jnp.bfloat16)
    seq_queries = split_seqs(query_heads, seq_count)
    seq_keys = split_seqs(key_heads, seq_count)
    seq_values = split_seqs(value_heads, seq_count)
    seq_segments = split_seqs(segments, seq_count)
    attended, log_total = lax.map(attend, (seq_queries, seq_keys, seq_values, seq_segments))
    attended_low = attended.reshape(row_count, D)
    residual = hidden_in + jnp.dot(attended_low, out_low, preferred_element_type=jnp.float32)
    normed_two, norm_back_two = jax.vjp(layer_norm, residual, gains_full[1])
    normed_two_low = normed_two.astype(jnp.bfloat16)
    gate_up = jnp.dot(normed_two_low, in_low, preferred_element_type=jnp.float32)
    active, geglu_back = jax.vjp(geglu, gate_up)
    active_low = active.astype(jnp.bfloat16)
    output = residual + jnp.dot(active_low, down_low, preferred_element_type=jnp.float32)
    activations = output.astype(jnp.bfloat16)
    gathered_back = (
        lax.all_gather(rounded[0], "fsdp", axis=0, tiled=True),
        lax.all_gather(rounded[1], "fsdp", axis=0, tiled=True),
        lax.all_gather(rounded[2], "fsdp", axis=0, tiled=True),
        lax.all_gather(rounded[3], "fsdp", axis=0, tiled=True),
        lax.all_gather(rounded[4], "fsdp", axis=1, tiled=True),
    )
    qkv_low, out_low, in_low, down_low, gains_low = gathered_back
    grad_down = jnp.dot(active_low.T, cotangent, preferred_element_type=jnp.float32)
    grad_active = jnp.dot(cotangent, down_low.T, preferred_element_type=jnp.float32)
    grad_gate_up = geglu_back(grad_active)[0].astype(jnp.bfloat16)
    grad_in = jnp.dot(normed_two_low.T, grad_gate_up, preferred_element_type=jnp.float32)
    grad_normed_two = jnp.dot(grad_gate_up, in_low.T, preferred_element_type=jnp.float32)
    grad_resid_norm, gain_two_grad = norm_back_two(grad_normed_two)
    grad_residual = cotangent.astype(jnp.float32) + grad_resid_norm
    grad_residual_low = grad_residual.astype(jnp.bfloat16)
    grad_outw = jnp.dot(attended_low.T, grad_residual_low, preferred_element_type=jnp.float32)
    grad_attended = jnp.dot(
        grad_residual_low, out_low.T, preferred_element_type=jnp.float32
    ).astype(jnp.bfloat16)
    seq_grad_heads = split_seqs(grad_attended.reshape(row_count, HEADS, HEAD), seq_count)
    grad_queries, grad_keys, grad_values = lax.map(
        attend_back, (seq_queries, seq_keys, seq_values, seq_grad_heads, log_total, seq_segments)
    )
    grad_queries = rotate(grad_queries.reshape(row_count, HEADS, HEAD), cosine, -sine)
    grad_keys = rotate(grad_keys.reshape(row_count, HEADS, HEAD), cosine, -sine)
    grad_mixed = jnp.concatenate(
        [
            grad_queries.reshape(row_count, D),
            grad_keys.reshape(row_count, D),
            grad_values.reshape(row_count, D),
        ],
        axis=1,
    ).astype(jnp.bfloat16)
    grad_qkv = jnp.dot(normed_low.T, grad_mixed, preferred_element_type=jnp.float32)
    grad_normed = jnp.dot(grad_mixed, qkv_low.T, preferred_element_type=jnp.float32)
    grad_input_norm, gain_one_grad = norm_back_one(grad_normed)
    input_grad = grad_residual + grad_input_norm
    gain_pair_grad = jnp.stack([gain_one_grad, gain_two_grad])
    owned_qkv, owned_out, owned_in, owned_down, owned_gain = (
        lax.psum_scatter(grad_qkv, "fsdp", scatter_dimension=0, tiled=True),
        lax.psum_scatter(grad_outw, "fsdp", scatter_dimension=0, tiled=True),
        lax.psum_scatter(grad_in, "fsdp", scatter_dimension=0, tiled=True),
        lax.psum_scatter(grad_down, "fsdp", scatter_dimension=0, tiled=True),
        lax.psum_scatter(gain_pair_grad, "fsdp", scatter_dimension=1, tiled=True),
    )
    qkv_state = adam_step(qkv_weight, owned_qkv, qkv_first, qkv_second)
    out_state = adam_step(out_weight, owned_out, out_first, out_second)
    in_state = adam_step(in_weight, owned_in, in_first, in_second)
    down_state = adam_step(down_weight, owned_down, down_first, down_second)
    gains_state = adam_step(norm_gains, owned_gain, gains_first, gains_second)
    gains_delta = gains_state[1] - norm_gains
    return (
        activations,
        input_grad,
        qkv_state[0],
        qkv_state[1],
        qkv_state[2],
        qkv_state[3],
        out_state[0],
        out_state[1],
        out_state[2],
        out_state[3],
        in_state[0],
        in_state[1],
        in_state[2],
        in_state[3],
        down_state[0],
        down_state[1],
        down_state[2],
        down_state[3],
        gains_state[0],
        gains_delta,
        gains_state[2],
        gains_state[3],
    )


def solution(mesh):
    return jax.shard_map(
        shards,
        mesh=mesh,
        in_specs=(
            P("fsdp", None),
            P("fsdp", None),
            P("fsdp"),
            P("fsdp"),
            P("fsdp", None),
            P("fsdp", None),
            P("fsdp", None),
            P("fsdp", None),
            P("fsdp", None),
            P("fsdp", None),
            P("fsdp", None),
            P("fsdp", None),
            P("fsdp", None),
            P("fsdp", None),
            P("fsdp", None),
            P("fsdp", None),
            P(None, "fsdp"),
            P(None, "fsdp"),
            P(None, "fsdp"),
        ),
        out_specs=(
            P("fsdp", None),
            P("fsdp", None),
            P("fsdp", None),
            P("fsdp", None),
            P("fsdp", None),
            P("fsdp", None),
            P("fsdp", None),
            P("fsdp", None),
            P("fsdp", None),
            P("fsdp", None),
            P("fsdp", None),
            P("fsdp", None),
            P("fsdp", None),
            P("fsdp", None),
            P("fsdp", None),
            P("fsdp", None),
            P("fsdp", None),
            P("fsdp", None),
            P(None, "fsdp"),
            P(None, "fsdp"),
            P(None, "fsdp"),
            P(None, "fsdp"),
        ),
        check_vma=False,
    )
```

profile of v0, /device:TPU:0, one launch (start us, length us, event | category | flops | bytes accessed | tf_op | source)
XLA Modules:
  0.0 1512.9 jit_solution(8953548538941148751)
XLA Ops:
  18.5 43.1 %all-gather = bf16[32,24,2]{1,2,0:T(2,128)(2,1)S(1)} all-gather(bf16[1,24,2]{1,2,0:T(2,128)(2,1)S(1)} %convert_bitcast_fusion.1), channel_id=1, replica_groups=mesh['fsdp'=32] {'fsdp'}, dimensions={0}, use_global_device_ids=true | all-gather | bytes 3168 | tf_op jit(solution)/shard_map/all_gather | solution.py:179
  75.7 57.1 %all-gather.7.cloned.1.call-done = bf16[768,2304]{1,0:T(8,128)(2,1)} async-done(((bf16[24,2304]{1,0:T(8,128)(2,1)}), bf16[768,2304]{1,0:T(8,128)(2,1)}) %all-gather.7.cloned.1.call-update) | async-done | bytes 3538960 | tf_op jit(solution)/shard_map/all_gather | solution.py:175
  132.8 13.6 fusion.103
  146.4 10.2 fusion.135
  159.7 6.6 copy.175
  166.3 8.4 reshape.589
  174.7 6.5 slice_negate_fusion.3
  191.7 6.6 copy.177
  198.4 8.4 reshape.591
  206.8 6.4 slice_negate_fusion.2
  213.2 5.6 concatenate.185
  218.8 5.3 concatenate.186
  224.1 10.3 fusion.94
  242.1 6.1 convert_element_type.113
  250.9 250.1 %while.30 = (s32[]{:T(128)}, bf16[4,512,12,64]{1,3,2,0:T(8,128)(2,1)}, f32[4,4,12,128,1]{3,2,1,4,0:T(8,128)}, bf16[4,512,12,64]{1,3,2,0:T(8,128)(2,1)S(1)}, s32[...) while((s32[]{:T(128)}, ...), condition=%wide.region_5.6_spmd, body=%wide.region_2.5_spmd.sunk | while | flops 657465344 | bytes 106623328 | solution.py:201
  301.4 6.1 fusion.187
  363.9 6.1 fusion.187
  426.4 6.1 fusion.187
  488.8 6.1 fusion.187
  501.0 5.5 copy.182
  509.2 6.0 fusion.136
  518.7 11.3 fusion.121
  530.0 26.2 %fusion.98 = (f32[2048,1152]{1,0:T(8,128)}, f32[2048,1152]{1,0:T(8,128)}, f32[2048,1152]{1,0:T(8,128)}) fusion(f32[2048,2304]{1,0:T(8,128)S(1)} %fusion.121, bf16[2048,768]{1,0:T(8,128)(2,1)S(1)} %copy-done.19, bf16[1152,768]{1,0:T(8,128)(2,1)S(1)} %copy-done.25), kind=kOutput, calls=%fused_computation.188 | convolution fusion | flops 3777232896 | bytes 42663936 | tf_op jit(solution)/shard_map/dot_general | solution.py:220
  556.2 14.6 multiply_add_fusion
  570.7 16.2 %multiply_reduce_fusion.1 = (f32[768]{0:T(1024)}, f32[2048]{0:T(1024)S(1)}, f32[2048,768]{0,1:T(8,128)}) fusion(f32[2048,768]{0,1:T(8,128)} %copy-done.10, f32[2048]{0:T(1024)S(1)} %fusion.115, f32[2048]{0:T(1024)S(1)} %broadcast_multiply_fusion.2, f32[768]{0:T(1024)S(1)} %copy-done.41, bf16[768,2304]{1,0:T(8,128)(2,1)} %all-gather.11.cloned.1.call-done, ...), kind=kOutput, calls=%fused_computation.173 | convolution fusion | flops 7268201472 | bytes 35026944 | tf_op jit(solution)/shard_map/dot_general | solution.py:223
  587.0 5.8 fusion.127
  604.3 5.3 convolution_convert_fusion
  621.2 19.0 %fusion.99 = f32[768,2304]{1,0:T(8,128)} fusion(f32[2048,1152]{1,0:T(8,128)} %get-tuple-element.515, f32[2048,1152]{1,0:T(8,128)} %get-tuple-element.463, f32[2048,768]{0,1:T(8,128)} %copy-done.10, f32[768]{0:T(1024)S(1)} %copy-done.41, f32[2048]{0:T(1024)S(1)} %fusion.115, f32[2048]{0:T(1024)S(1)} %broadcast_multiply_fusion.2), kind=kOutput, calls=%fused_computation.189 | convolution fusion | flops 7263485952 | bytes 32263168 | tf_op jit(solution)/shard_map/dot_general | solution.py:222
  642.0 588.1 %while.31 = (s32[]{:T(128)}, f32[4,512,12,64]{1,0,3,2:T(4,128)}, f32[4,512,12,64]{1,0,3,2:T(4,128)}, bf16[4,512,12,64]{1,3,2,0:T(8,128)(2,1)}, bf16[4,512,12,64]...) while((s32[]{:T(128)}, f32[4,512,12,64]{1,0,3,2:T(4,128)}, ...), condition=%wide.region_12.13_spmd, body=%wide.region_10.12_spmd.sunk | while | flops 1587027968 | bytes 218263584 | solution.py:232
  666.4 6.8 fusion.194
  679.7 5.4 fusion.201
  705.2 6.7 multiply_reduce_fusion.5
  719.8 31.3 %dynamic_update_slice.45 = f32[4,512,12,64]{1,0,3,2:T(4,128)} dynamic-update-slice(f32[4,512,12,64]{1,0,3,2:T(4,128)} %get-tuple-element.790, f32[1,512,12,64]{1,0,3,2:T(1,128)} %bitcast.205, s32[]{:T(128)} %get-tuple-element.788, s32[]{:T(128)} %constant.218.clone.1..sunk.1, s32[]{:T(128)} %constant.218.clone.1..sunk.1, s32[]{:T(128)} %constant.218.clone.1..sunk.1) | dynamic-update-slice | bytes 3145732 | tf_op jit(solution)/shard_map/while/body/jit(dynamic_update_index_in_dim)/dynamic_update_slice | solution.py:232
  758.4 31.2 %dynamic_update_slice.44 = f32[4,512,12,64]{1,0,3,2:T(4,128)} dynamic-update-slice(f32[4,512,12,64]{1,0,3,2:T(4,128)} %get-tuple-element.789, f32[1,512,12,64]{1,0,3,2:T(1,128)} %bitcast.204, s32[]{:T(128)} %get-tuple-element.788, s32[]{:T(128)} %constant.218.clone.1..sunk.1, s32[]{:T(128)} %constant.218.clone.1..sunk.1, s32[]{:T(128)} %constant.218.clone.1..sunk.1) | dynamic-update-slice | bytes 3145732 | tf_op jit(solution)/shard_map/while/body/jit(dynamic_update_index_in_dim)/dynamic_update_slice | solution.py:232
  813.5 6.8 fusion.194
  826.8 5.3 fusion.201
  852.3 6.7 multiply_reduce_fusion.5
  866.9 31.0 %dynamic_update_slice.45 = f32[4,512,12,64]{1,0,3,2:T(4,128)} dynamic-update-slice(f32[4,512,12,64]{1,0,3,2:T(4,128)} %get-tuple-element.790, f32[1,512,12,64]{1,0,3,2:T(1,128)} %bitcast.205, s32[]{:T(128)} %get-tuple-element.788, s32[]{:T(128)} %constant.218.clone.1..sunk.1, s32[]{:T(128)} %constant.218.clone.1..sunk.1, s32[]{:T(128)} %constant.218.clone.1..sunk.1) | dynamic-update-slice | bytes 3145732 | tf_op jit(solution)/shard_map/while/body/jit(dynamic_update_index_in_dim)/dynamic_update_slice | solution.py:232
  905.3 31.0 %dynamic_update_slice.44 = f32[4,512,12,64]{1,0,3,2:T(4,128)} dynamic-update-slice(f32[4,512,12,64]{1,0,3,2:T(4,128)} %get-tuple-element.789, f32[1,512,12,64]{1,0,3,2:T(1,128)} %bitcast.204, s32[]{:T(128)} %get-tuple-element.788, s32[]{:T(128)} %constant.218.clone.1..sunk.1, s32[]{:T(128)} %constant.218.clone.1..sunk.1, s32[]{:T(128)} %constant.218.clone.1..sunk.1) | dynamic-update-slice | bytes 3145732 | tf_op jit(solution)/shard_map/while/body/jit(dynamic_update_index_in_dim)/dynamic_update_slice | solution.py:232
  960.3 6.8 fusion.194
  973.5 5.3 fusion.201
  999.1 6.7 multiply_reduce_fusion.5
  1013.7 31.0 %dynamic_update_slice.45 = f32[4,512,12,64]{1,0,3,2:T(4,128)} dynamic-update-slice(f32[4,512,12,64]{1,0,3,2:T(4,128)} %get-tuple-element.790, f32[1,512,12,64]{1,0,3,2:T(1,128)} %bitcast.205, s32[]{:T(128)} %get-tuple-element.788, s32[]{:T(128)} %constant.218.clone.1..sunk.1, s32[]{:T(128)} %constant.218.clone.1..sunk.1, s32[]{:T(128)} %constant.218.clone.1..sunk.1) | dynamic-update-slice | bytes 3145732 | tf_op jit(solution)/shard_map/while/body/jit(dynamic_update_index_in_dim)/dynamic_update_slice | solution.py:232
  1052.1 31.0 %dynamic_update_slice.44 = f32[4,512,12,64]{1,0,3,2:T(4,128)} dynamic-update-slice(f32[4,512,12,64]{1,0,3,2:T(4,128)} %get-tuple-element.789, f32[1,512,12,64]{1,0,3,2:T(1,128)} %bitcast.204, s32[]{:T(128)} %get-tuple-element.788, s32[]{:T(128)} %constant.218.clone.1..sunk.1, s32[]{:T(128)} %constant.218.clone.1..sunk.1, s32[]{:T(128)} %constant.218.clone.1..sunk.1) | dynamic-update-slice | bytes 3145732 | tf_op jit(solution)/shard_map/while/body/jit(dynamic_update_index_in_dim)/dynamic_update_slice | solution.py:232
  1107.0 6.8 fusion.194
  1120.3 5.3 fusion.201
  1145.8 6.7 multiply_reduce_fusion.5
  1160.4 31.0 %dynamic_update_slice.45 = f32[4,512,12,64]{1,0,3,2:T(4,128)} dynamic-update-slice(f32[4,512,12,64]{1,0,3,2:T(4,128)} %get-tuple-element.790, f32[1,512,12,64]{1,0,3,2:T(1,128)} %bitcast.205, s32[]{:T(128)} %get-tuple-element.788, s32[]{:T(128)} %constant.218.clone.1..sunk.1, s32[]{:T(128)} %constant.218.clone.1..sunk.1, s32[]{:T(128)} %constant.218.clone.1..sunk.1) | dynamic-update-slice | bytes 3145732 | tf_op jit(solution)/shard_map/while/body/jit(dynamic_update_index_in_dim)/dynamic_update_slice | solution.py:232
  1198.7 31.0 %dynamic_update_slice.44 = f32[4,512,12,64]{1,0,3,2:T(4,128)} dynamic-update-slice(f32[4,512,12,64]{1,0,3,2:T(4,128)} %get-tuple-element.789, f32[1,512,12,64]{1,0,3,2:T(1,128)} %bitcast.204, s32[]{:T(128)} %get-tuple-element.788, s32[]{:T(128)} %constant.218.clone.1..sunk.1, s32[]{:T(128)} %constant.218.clone.1..sunk.1, s32[]{:T(128)} %constant.218.clone.1..sunk.1) | dynamic-update-slice | bytes 3145732 | tf_op jit(solution)/shard_map/while/body/jit(dynamic_update_index_in_dim)/dynamic_update_slice | solution.py:232
  1230.2 8.5 reshape.595
  1238.7 8.6 reshape.597
  1247.3 8.7 copy.217
  1256.0 5.7 copy.218
  1266.9 9.3 slice_negate_fusion
  1276.1 6.6 maximum_multiply_fusion.2
  1282.8 8.5 fusion.88
  1291.3 14.2 fusion.96
  1305.6 9.1 fusion.138
  1314.7 89.5 %fusion = f32[40,768]{1,0:T(8,128)S(1)} fusion(f32[1152,768]{1,0:T(8,128)} %fusion.138), kind=kCustom, calls=%all-reduce-scatter | all-reduce-scatter fusion | flops 983041 | bytes 3661824
  1410.0 11.3 fusion.86
  1428.5 38.5 %all-reduce.3 = f32[2,768]{1,0:T(2,128)S(1)} all-reduce(f32[2,768]{1,0:T(2,128)S(1)} %pad_maximum_fusion.5), channel_id=6, replica_groups=mesh['fsdp'=32] {'fsdp'}, use_global_device_ids=true, to_apply=%region_21.22.clone | all-reduce | flops 1536 | bytes 12288
  1467.0 10.8 add_convert_fusion.1
  1477.8 6.7 add_add_fusion.4
  1485.3 6.7 copy.196
  (581 shorter events, 600.2 us)
Async XLA Ops:
  7.2 64.9 %all-gather.13.cloned.1.call-start = ((), (), s32[]{:S(2)}) async-start(), calls=%async_computation.9 | async-start | bytes 2027520 | tf_op jit(solution)/shard_map/all_gather | solution.py:178
  8.8 123.9 %all-gather.7.cloned.1.call-start = ((), (), s32[]{:S(2)}) async-start(), calls=%async_computation.3 | async-start | bytes 3649536 | tf_op jit(solution)/shard_map/all_gather | solution.py:175
  10.5 498.7 %all-gather.9.cloned.1.call-start = ((), (), s32[]{:S(2)}) async-start(), calls=%async_computation.4 | async-start | bytes 1216512 | tf_op jit(solution)/shard_map/all_gather | solution.py:176
  12.0 506.6 %all-gather.11.cloned.1.call-start = ((), (), s32[]{:S(2)}) async-start(), calls=%async_computation.5 | async-start | bytes 3649536 | tf_op jit(solution)/shard_map/all_gather | solution.py:177
  13.7 1486.1 %reduce-scatter.9.cloned.1.call-start = ((), (), s32[]{:S(2)}) async-start(), calls=%async_computation.7 | async-start | bytes 2433024 | tf_op jit(solution)/shard_map/reduce_scatter | solution.py:252
  13.8 48.7 %copy-start.45 = (f32[32]{0:T(128)}, f32[32]{0:T(128)S(1)}, u32[]{:S(2)}) copy-start(f32[32]{0:T(128)S(1)} %negate_power_fusion) | copy-start | bytes 388
  13.9 48.6 %copy-start.42 = (s32[2048]{0:T(1024)S(1)}, s32[2048]{0:T(1024)}, u32[]{:S(2)}) copy-start(s32[2048]{0:T(1024)} %param.26) | copy-start | bytes 24580
  13.9 53.4 %copy-start.43 = (s32[2048]{0:T(1024)S(1)}, s32[2048]{0:T(1024)}, u32[]{:S(2)}) copy-start(s32[2048]{0:T(1024)} %param.25) | copy-start | bytes 24580
  17.1 115.7 %copy-start.5 = (bf16[2048,768]{0,1:T(8,128)(2,1)}, bf16[2048,768]{0,1:T(8,128)(2,1)S(1)}, u32[]{:S(2)}) copy-start(bf16[2048,768]{0,1:T(8,128)(2,1)S(1)} %copy.171) | copy-start | bytes 9437188
  17.6 115.2 %copy-start.29 = (f32[2048]{0:T(1024)}, f32[2048]{0:T(1024)S(1)}, u32[]{:S(2)}) copy-start(f32[2048]{0:T(1024)S(1)} %broadcast_multiply_fusion.3) | copy-start | bytes 24580
  18.5 43.1 %copy-start.35 = (f32[2048]{0:T(1024)}, f32[2048]{0:T(1024)S(1)}, u32[]{:S(2)}) copy-start(f32[2048]{0:T(1024)S(1)} %fusion.85) | copy-start | bytes 24580
  18.5 127.9 %copy-start.31 = (f32[2048]{0:T(1024)}, f32[2048]{0:T(1024)S(1)}, u32[]{:S(2)}) copy-start(f32[2048]{0:T(1024)S(1)} %fusion.114) | copy-start | bytes 24580
  62.5 83.9 %copy-start.39 = (f32[768]{0:T(1024)}, f32[768]{0:T(1024)S(1)}, u32[]{:S(2)}) copy-start(f32[768]{0:T(1024)S(1)} %get-tuple-element.409) | copy-start | bytes 9220
  62.5 83.9 %copy-start.37 = (f32[2048]{0:T(1024)}, f32[2048]{0:T(1024)S(1)}, u32[]{:S(2)}) copy-start(f32[2048]{0:T(1024)S(1)} %convert_element_type.114) | copy-start | bytes 24580
  279.7 6.9 copy-start.17
  342.1 6.9 copy-start.17
  404.6 6.9 copy-start.17
  467.0 6.9 copy-start.17
  501.0 8.2 copy-start.2
  501.0 8.2 copy-start.27
  518.6 11.3 copy-start.19
  518.7 11.3 copy-start.25
  601.0 900.5 %reduce-scatter.11.cloned.1.call-start = ((), (), s32[]{:S(2)}) async-start(), calls=%async_computation.8 | async-start | bytes 7299072 | tf_op jit(solution)/shard_map/reduce_scatter | solution.py:253
  640.2 863.4 %reduce-scatter.7.cloned.1.call-start = ((), (), s32[]{:S(2)}) async-start(), calls=%async_computation.6 | async-start | bytes 7299072 | tf_op jit(solution)/shard_map/reduce_scatter | solution.py:251
  656.5 16.7 %copy-start.13 = (bf16[1,128,12,64]{1,3,2,0:T(8,128)(2,1)}, bf16[1,128,12,64]{1,3,2,0:T(8,128)(2,1)S(1)}, u32[]{:S(2)}) copy-start(bf16[1,128,12,64]{1,3,2,0:T(8,128)(2,1)S(1)} %get-tuple-element.714) | copy-start | bytes 589828 | tf_op jit(solution)/shard_map/while
  703.7 8.3 slice-start
  705.2 6.8 slice-start.1
  705.2 6.8 slice-start.2
  705.2 6.8 copy-start.16
  717.1 33.9 %copy-start.14 = (bf16[1,128,12,64]{1,3,2,0:T(8,128)(2,1)S(1)}, bf16[1,128,12,64]{1,3,2,0:T(8,128)(2,1)}, u32[]{:S(2)}) copy-start(bf16[1,128,12,64]{1,3,2,0:T(8,128)(2,1)} %copy-done.13) | copy-start | bytes 589828 | tf_op jit(solution)/shard_map/while
  803.7 16.6 %copy-start.13 = (bf16[1,128,12,64]{1,3,2,0:T(8,128)(2,1)}, bf16[1,128,12,64]{1,3,2,0:T(8,128)(2,1)S(1)}, u32[]{:S(2)}) copy-start(bf16[1,128,12,64]{1,3,2,0:T(8,128)(2,1)S(1)} %get-tuple-element.714) | copy-start | bytes 589828 | tf_op jit(solution)/shard_map/while
  850.8 8.3 slice-start
  852.3 6.8 slice-start.1
  852.3 6.8 slice-start.2
  852.3 6.8 copy-start.16
  864.2 33.7 %copy-start.14 = (bf16[1,128,12,64]{1,3,2,0:T(8,128)(2,1)S(1)}, bf16[1,128,12,64]{1,3,2,0:T(8,128)(2,1)}, u32[]{:S(2)}) copy-start(bf16[1,128,12,64]{1,3,2,0:T(8,128)(2,1)} %copy-done.13) | copy-start | bytes 589828 | tf_op jit(solution)/shard_map/while
  950.5 16.6 %copy-start.13 = (bf16[1,128,12,64]{1,3,2,0:T(8,128)(2,1)}, bf16[1,128,12,64]{1,3,2,0:T(8,128)(2,1)S(1)}, u32[]{:S(2)}) copy-start(bf16[1,128,12,64]{1,3,2,0:T(8,128)(2,1)S(1)} %get-tuple-element.714) | copy-start | bytes 589828 | tf_op jit(solution)/shard_map/while
  997.6 8.3 slice-start
  999.1 6.8 slice-start.1
  999.1 6.8 slice-start.2
  999.1 6.8 copy-start.16
  1011.0 33.7 %copy-start.14 = (bf16[1,128,12,64]{1,3,2,0:T(8,128)(2,1)S(1)}, bf16[1,128,12,64]{1,3,2,0:T(8,128)(2,1)}, u32[]{:S(2)}) copy-start(bf16[1,128,12,64]{1,3,2,0:T(8,128)(2,1)} %copy-done.13) | copy-start | bytes 589828 | tf_op jit(solution)/shard_map/while
  1097.2 16.6 %copy-start.13 = (bf16[1,128,12,64]{1,3,2,0:T(8,128)(2,1)}, bf16[1,128,12,64]{1,3,2,0:T(8,128)(2,1)S(1)}, u32[]{:S(2)}) copy-start(bf16[1,128,12,64]{1,3,2,0:T(8,128)(2,1)S(1)} %get-tuple-element.714) | copy-start | bytes 589828 | tf_op jit(solution)/shard_map/while
  1144.3 8.3 slice-start
  1145.8 6.8 slice-start.1
  1145.8 6.8 slice-start.2
  1157.7 33.7 %copy-start.14 = (bf16[1,128,12,64]{1,3,2,0:T(8,128)(2,1)S(1)}, bf16[1,128,12,64]{1,3,2,0:T(8,128)(2,1)}, u32[]{:S(2)}) copy-start(bf16[1,128,12,64]{1,3,2,0:T(8,128)(2,1)} %copy-done.13) | copy-start | bytes 589828 | tf_op jit(solution)/shard_map/while
  1238.7 17.3 %slice-start.3 = ((s8[6291456]{0:T(1024)(128)(4,1)}), s8[2097152]{0:T(1024)(128)(4,1)S(1)}, s32[]{:S(2)}) async-start(s8[6291456]{0:T(1024)(128)(4,1)} %bitcast.209), calls=%async_computation.13 | async-start | bytes 4194304
  1247.3 8.7 slice-start.4
  1266.9 9.3 copy-start.24
  1266.9 15.9 %slice-start.5 = ((s8[6291456]{0:T(1024)(128)(4,1)}), s8[2097152]{0:T(1024)(128)(4,1)S(1)}, s32[]{:S(2)}) async-start(s8[6291456]{0:T(1024)(128)(4,1)} %bitcast.212), calls=%async_computation.15 | async-start | bytes 4194304
  1282.8 8.5 copy-start.6
  1282.8 8.5 copy-start.30
  1282.8 8.5 copy-start.32
  1282.8 8.5 copy-start.40
  1404.2 90.6 %collective-permute-start = (f32[40,768]{1,0:T(8,128)S(1)}, f32[40,768]{1,0:T(8,128)}, u32[]{:S(2)}, u32[]{:S(2)}) collective-permute-start(f32[40,768]{1,0:T(8,128)S(1)} %fusion), channel_id=1, source_target_pairs={{0,1},{1,2},{2,3},{3,4},{4,5},{5,6},{6,7},{7,8},{8,9},{9,10},{10,1... | collective-permute-start | bytes 368648
  1406.1 88.6 %collective-permute-start.1 = (f32[40,768]{1,0:T(8,128)S(1)}, f32[40,768]{1,0:T(8,128)}, u32[]{:S(2)}, u32[]{:S(2)}) collective-permute-start(f32[40,768]{1,0:T(8,128)S(1)} %fusion), channel_id=1, source_target_pairs={{0,2},{1,3},{2,4},{3,5},{4,6},{5,7},{6,8},{7,9},{8,10},{9,11},{10,... | collective-permute-start | bytes 368648
  1408.1 86.7 %collective-permute-start.2 = (f32[40,768]{1,0:T(8,128)S(1)}, f32[40,768]{1,0:T(8,128)}, u32[]{:S(2)}, u32[]{:S(2)}) collective-permute-start(f32[40,768]{1,0:T(8,128)S(1)} %fusion), channel_id=1, source_target_pairs={{0,3},{1,4},{2,5},{3,6},{4,7},{5,8},{6,9},{7,10},{8,11},{9,12},{10... | collective-permute-start | bytes 368648
  1410.0 11.3 copy-start.36
  1427.2 67.6 %collective-permute-start.3 = (f32[4,768]{1,0:T(4,128)S(1)}, f32[4,768]{1,0:T(4,128)S(1)}, u32[]{:S(2)}, u32[]{:S(2)}) collective-permute-start(f32[4,768]{1,0:T(4,128)S(1)} %slice.362), channel_id=1, source_target_pairs={{0,4},{1,5},{2,6},{3,7},{4,8},{5,9},{6,10},{7,11},{8,12},{9,13},{1... | collective-permute-start | bytes 36872
  1467.0 10.8 copy-start.9
  1467.0 10.8 copy-start.12
  1467.0 10.8 copy-start.34
  1492.0 9.5 copy-start.26
  (41 other events, 159.3 us)
Sparse Core Ops, SparseCore 0:
  11.5 58.8 all-gather.12
  73.8 58.8 all-gather.6
  136.2 52.8 all-gather.8
  192.4 59.0 all-gather.10
  601.1 97.8 reduce-scatter.8
  706.1 118.0 reduce-scatter.10
  1305.7 133.9 reduce-scatter.6
where the time goes:
time: 1530 us; the launch traced here: 1510 us
  local copies, waits for them, and re-layouts  834 us (55%)
  matrix products  287 us (19%)
  blocking collectives  171 us (11%)
  other arithmetic  139 us (9%)
  waiting for transfers between devices  57.2 us (4%)
    dynamic_update_slice x12, local copies, waits for them, and re-layouts, shards(): lax.map(attend_back, (seq_queries, seq_keys, seq_values, seq_grad_heads,...  257 us
    unnamed x2, blocking collectives  128 us
    slice x64, local copies, waits for them, and re-layouts, widen(): before = jnp.roll(blocked, 1, axis=0)  115 us
    slice x32, local copies, waits for them, and re-layouts, widen(): after = jnp.roll(blocked, -1, axis=0)  76 us
    all_gather x1, waiting for transfers between devices, shards(): lax.all_gather(rounded[0], 'fsdp', axis=0, tiled=True)  57.1 us
    unnamed x103, local copies, waits for them, and re-layouts  54.2 us
    all_gather x1, blocking collectives, shards(): lax.all_gather(rounded[4], 'fsdp', axis=1, tiled=True)  43.1 us
    dot_general x8, matrix products, block_scores(): jnp.einsum('bqhe,bkhe->bhqk', query_blocks, key_wide, preferred_element_t...  42.9 us
  transfers between devices with their start and end apart: 11, of which 1 were waited for; matrix products, arithmetic and copies ran while one was open for 82% of the time, Pallas kernels for 0%

commit v1 on v0

v1 whole, which is shorter than its diff:
```python
import jax
import jax.numpy as jnp
from jax import lax
from jax.experimental import pallas as pl
from jax.experimental.pallas import tpu as pltpu
from jax.sharding import PartitionSpec as P

D = 768
HEADS = 12
HEAD = 64
FF = 1152
SEQ = 512
BLK = 128
STEP = 10

NORM_EPS = 1e-05
BETA_ONE = 0.9
BETA_TWO = 0.98
ADAM_EPS = 1e-06
LEARN_RATE = 0.1
WEIGHT_DECAY = 0.01
ROPE_BASE = 10000.0
MASKED = -1e30

GROUP = 4
WIDE = GROUP * HEAD
GROUPS = HEADS // GROUP
BLOCKS = SEQ // BLK
SPAN = 2 * BLK
KEY_AT = tuple(min(max(b * BLK - BLK // 2, 0), SEQ - SPAN) for b in range(BLOCKS))
FF_CHUNKS = ((0, 256), (256, 256), (512, 256), (768, 256), (1024, 128))
VMEM = 60 * 1024 * 1024
BF = jnp.bfloat16
F32 = jnp.float32


def mm(a, b):
    return lax.dot_general(a, b, (((1,), (0,)), ((), ())), preferred_element_type=F32)


def mm_nt(a, b):
    return lax.dot_general(a, b, (((1,), (1,)), ((), ())), preferred_element_type=F32)


def mm_tn(a, b):
    return lax.dot_general(a, b, (((0,), (0,)), ((), ())), preferred_element_type=F32)


def norm_parts(x):
    center = x - jnp.mean(x, axis=-1, keepdims=True)
    scale = lax.rsqrt(jnp.mean(center * center, axis=-1, keepdims=True) + NORM_EPS)
    return center * scale, scale


def norm_back(e, gain, xh, scale):
    f = e * gain
    return (
        f - jnp.mean(f, axis=-1, keepdims=True) - xh * jnp.mean(f * xh, axis=-1, keepdims=True)
    ) * scale


def turned(u):
    half = HEAD // 2
    lane = lax.broadcasted_iota(jnp.int32, u.shape, 1)
    return jnp.where(
        lane % HEAD < half, pltpu.roll(u, u.shape[1] - half, 1), pltpu.roll(u, half, 1)
    )


def twice(t):
    return jnp.concatenate([t, t], axis=1)


def head_masks(dtype):
    lane = lax.broadcasted_iota(jnp.int32, (1, WIDE), 1)
    return [jnp.where(lane // HEAD == j, 1.0, 0.0).astype(dtype) for j in range(GROUP)]


def spread_heads(block, masks):
    return jnp.concatenate([block * m for m in masks], axis=0)


def gather_heads(stacked, masks):
    total = stacked[:BLK] * masks[0]
    for j in range(1, GROUP):
        total = total + stacked[j * BLK : (j + 1) * BLK] * masks[j]
    return total


def fill_bias(segc_ref, segr_ref, bias_ref):
    for b in range(BLOCKS):
        ks = KEY_AT[b]
        key_at = ks + lax.broadcasted_iota(jnp.int32, (SPAN, BLK), 0)
        query_at = b * BLK + lax.broadcasted_iota(jnp.int32, (SPAN, BLK), 1)
        near = jnp.abs(key_at - query_at) <= BLK // 2
        same = segc_ref[ks : ks + SPAN, :] == segr_ref[0, :, b * BLK : (b + 1) * BLK]
        bias_ref[b] = jnp.where(near & same, 0.0, MASKED)


def bias_of(bias_ref, b):
    one = bias_ref[b]
    return jnp.concatenate([one] * GROUP, axis=1)


def attend_kernel(
    tok_ref, gain_ref, wqkv_ref, wo_ref, cos_ref, sin_ref, segc_ref, segr_ref,
    q_ref, k_ref, v_ref, att_ref, lse_ref, res_ref, bias_ref, normed_ref,
):
    xh, _ = norm_parts(tok_ref[...].astype(F32))
    normed_ref[...] = (xh * gain_ref[...]).astype(BF)
    fill_bias(segc_ref, segr_ref, bias_ref)
    masks_low, masks = head_masks(BF), head_masks(F32)

    def group(g, carry):
        at = pl.multiple_of(g * WIDE, WIDE)
        cosine, sine = twice(cos_ref[...]), twice(sin_ref[...])
        normed = normed_ref[...]
        u = mm(normed, wqkv_ref[:, pl.ds(at, WIDE)])
        q_ref[:, pl.ds(at, WIDE)] = (
            (u * cosine + turned(u) * sine) * HEAD ** (-0.5)
        ).astype(BF)
        u = mm(normed, wqkv_ref[:, pl.ds(D + at, WIDE)])
        k_ref[:, pl.ds(at, WIDE)] = (u * cosine + turned(u) * sine).astype(BF)
        v_ref[:, pl.ds(at, WIDE)] = mm(normed, wqkv_ref[:, pl.ds(2 * D + at, WIDE)]).astype(BF)
        for b in range(BLOCKS):
            ks, qs = KEY_AT[b], b * BLK
            heads_q = spread_heads(q_ref[qs : qs + BLK, pl.ds(at, WIDE)], masks_low)
            keys = k_ref[ks : ks + SPAN, pl.ds(at, WIDE)]
            vals = v_ref[ks : ks + SPAN, pl.ds(at, WIDE)]
            scores = mm_nt(keys, heads_q) + bias_of(bias_ref, b)
            top = jnp.max(scores, axis=0, keepdims=True)
            grown = jnp.exp(scores - top)
            total = jnp.sum(grown, axis=0, keepdims=True)
            prob = (grown * (1.0 / total)).astype(BF)
            att_ref[qs : qs + BLK, pl.ds(at, WIDE)] = gather_heads(
                mm_tn(prob, vals), masks
            ).astype(BF)
            lse_ref[g * BLOCKS + b] = top + jnp.log(total)
        return carry

    lax.fori_loop(0, GROUPS, group, 0)
    res_ref[...] = tok_ref[...].astype(F32) + mm(att_ref[...], wo_ref[...])


def feed_kernel(
    res_ref, cot_ref, gain_ref, wi_ref, wd_ref,
    act_ref, dres_ref, gin_ref, gdown_ref, ggain_ref,
    n2_ref, n2t_ref, out_ref, gn_ref, gin_acc, gdown_acc,
):
    step = pl.program_id(0)

    @pl.when(step == 0)
    def _():
        gin_acc[...] = jnp.zeros_like(gin_acc)
        gdown_acc[...] = jnp.zeros_like(gdown_acc)
        ggain_ref[...] = jnp.zeros_like(ggain_ref)

    xh, _ = norm_parts(res_ref[...])
    n2 = xh * gain_ref[...]
    n2_ref[...] = n2.astype(BF)
    n2t_ref[...] = n2.T.astype(BF)
    for i, (at, width) in enumerate(FF_CHUNKS):
        wi_gate = wi_ref[:, at : at + width]
        wi_up = wi_ref[:, FF + at : FF + at + width]
        wd = wd_ref[at : at + width, :]
        cot = cot_ref[...]
        gate = mm(n2_ref[...], wi_gate)
        up = mm(n2_ref[...], wi_up)
        phi = 0.5 + 0.5 * lax.erf(gate * (0.5**0.5))
        gelu = gate * phi
        active = gelu * up
        active_low = active.astype(BF)
        slope = phi + gate * jnp.exp(-0.5 * gate * gate) * 0.3989422804014327
        ga = mm_nt(cot, wd)
        dgate = (ga * up * slope).astype(BF)
        dup = (ga * gelu).astype(BF)
        out = mm(active_low, wd)
        gn = mm_nt(dgate, wi_gate) + mm_nt(dup, wi_up)
        if i == 0:
            out_ref[...] = out
            gn_ref[...] = gn
        else:
            out_ref[...] += out
            gn_ref[...] += gn
        gdown_acc[at : at + width, :] += mm_tn(active_low, cot)
        gin_acc[:, at : at + width] += mm(n2t_ref[...], dgate)
        gin_acc[:, FF + at : FF + at + width] += mm(n2t_ref[...], dup)
    res = res_ref[...]
    act_ref[...] = (res + out_ref[...]).astype(BF)
    xh, scale = norm_parts(res)
    gn = gn_ref[...]
    dres_ref[...] = cot_ref[...].astype(F32) + norm_back(gn, gain_ref[...], xh, scale)
    ggain_ref[...] += jnp.sum(gn * xh, axis=0, keepdims=True)

    @pl.when(step == pl.num_programs(0) - 1)
    def _():
        gin_ref[...] = gin_acc[...].astype(BF)
        gdown_ref[...] = gdown_acc[...].astype(BF)


def attend_back_kernel(
    dres_ref, tok_ref, gain_ref, wo_ref, cos_ref, sin_ref, segc_ref, segr_ref,
    q_ref, k_ref, v_ref, att_ref, lse_ref,
    gm_ref, gqkv_ref, gout_ref,
    bias_ref, normt_ref, ga_ref, dq_ref, dk_ref, dv_ref, gqkv_acc, gout_acc,
):
    step = pl.program_id(0)

    @pl.when(step == 0)
    def _():
        gqkv_acc[...] = jnp.zeros_like(gqkv_acc)
        gout_acc[...] = jnp.zeros_like(gout_acc)

    dres_low = dres_ref[...].astype(BF)
    ga_ref[...] = mm_nt(dres_low, wo_ref[...]).astype(BF)
    gout_acc[...] += mm_tn(att_ref[...], dres_low)
    xh, _ = norm_parts(tok_ref[...].astype(F32))
    normt_ref[...] = (xh * gain_ref[...]).T.astype(BF)
    fill_bias(segc_ref, segr_ref, bias_ref)
    masks_low, masks = head_masks(BF), head_masks(F32)

    def group(g, carry):
        at = pl.multiple_of(g * WIDE, WIDE)
        dk_ref[...] = jnp.zeros_like(dk_ref)
        dv_ref[...] = jnp.zeros_like(dv_ref)
        for b in range(BLOCKS):
            ks, qs = KEY_AT[b], b * BLK
            heads_q = spread_heads(q_ref[qs : qs + BLK, pl.ds(at, WIDE)], masks_low)
            heads_g = spread_heads(ga_ref[qs : qs + BLK, pl.ds(at, WIDE)], masks_low)
            keys = k_ref[ks : ks + SPAN, pl.ds(at, WIDE)]
            vals = v_ref[ks : ks + SPAN, pl.ds(at, WIDE)]
            scores = mm_nt(keys, heads_q) + bias_of(bias_ref, b)
            prob = jnp.exp(scores - lse_ref[g * BLOCKS + b])
            dv_ref[ks : ks + SPAN, :] += mm(prob.astype(BF), heads_g)
            dprob = mm_nt(vals, heads_g)
            inner = jnp.sum(prob * dprob, axis=0, keepdims=True)
            dscore = (prob * (dprob - inner)).astype(BF)
            dk_ref[ks : ks + SPAN, :] += mm(dscore, heads_q)
            dq_ref[qs : qs + BLK, :] = gather_heads(mm_tn(dscore, keys), masks)
        cosine, sine = twice(cos_ref[...]), twice(sin_ref[...])
        u = dq_ref[...] * HEAD ** (-0.5)
        part = (u * cosine - turned(u) * sine).astype(BF)
        gm_ref[:, pl.ds(at, WIDE)] = part
        gqkv_acc[:, pl.ds(at, WIDE)] += mm(normt_ref[...], part)
        u = dk_ref[...]
        part = (u * cosine - turned(u) * sine).astype(BF)
        gm_ref[:, pl.ds(D + at, WIDE)] = part
        gqkv_acc[:, pl.ds(D + at, WIDE)] += mm(normt_ref[...], part)
        part = dv_ref[...].astype(BF)
        gm_ref[:, pl.ds(2 * D + at, WIDE)] = part
        gqkv_acc[:, pl.ds(2 * D + at, WIDE)] += mm(normt_ref[...], part)
        return carry

    lax.fori_loop(0, GROUPS, group, 0)

    @pl.when(step == pl.num_programs(0) - 1)
    def _():
        gqkv_ref[...] = gqkv_acc[...].astype(BF)
        gout_ref[...] = gout_acc[...].astype(BF)


def input_kernel(gm_ref, tok_ref, dres_ref, gain_ref, wqkv_ref, gin_ref, ggain_ref):
    @pl.when(pl.program_id(0) == 0)
    def _():
        ggain_ref[...] = jnp.zeros_like(ggain_ref)

    xh, scale = norm_parts(tok_ref[...].astype(F32))
    e = mm_nt(gm_ref[...], wqkv_ref[...])
    gin_ref[...] = dres_ref[...] + norm_back(e, gain_ref[...], xh, scale)
    ggain_ref[...] += jnp.sum(e * xh, axis=0, keepdims=True)


def rows_of(width, height=SEQ):
    return pl.BlockSpec((height, width), lambda i: (i, 0))


def whole(*shape):
    return pl.BlockSpec(shape, lambda i: (0,) * len(shape), pipeline_mode=pl.Buffered(1))


def kept(*shape):
    return pl.BlockSpec(shape, lambda i: (0,) * len(shape))


def shape_of(shape, dtype):
    return jax.ShapeDtypeStruct(shape, dtype)


def run(kernel, steps, in_specs, out_specs, out_shape, scratch, flops, moved):
    return pl.pallas_call(
        kernel,
        grid=(steps,),
        in_specs=in_specs,
        out_specs=out_specs,
        out_shape=out_shape,
        scratch_shapes=scratch,
        cost_estimate=pl.CostEstimate(flops=flops, bytes_accessed=moved, transcendentals=0),
        compiler_params=pltpu.CompilerParams(
            dimension_semantics=("arbitrary",), vmem_limit_bytes=VMEM
        ),
    )


def rope_tables(places):
    half_dim = HEAD // 2
    frequency = ROPE_BASE ** (-(jnp.arange(half_dim).astype(F32) * 2.0 / HEAD))
    angles = places.astype(F32)[:, None] * frequency[None, :]
    cosine, sine = jnp.cos(angles), jnp.sin(angles)
    return (
        jnp.concatenate([cosine] * 4, axis=1),
        jnp.concatenate([-sine, sine, -sine, sine], axis=1),
    )


def adam_step(master, weight_grad, moment_one, moment_two):
    first_new = BETA_ONE * moment_one + (1.0 - BETA_ONE) * weight_grad
    second_new = BETA_TWO * moment_two + (1.0 - BETA_TWO) * weight_grad * weight_grad
    first_hat = first_new / (1.0 - BETA_ONE**STEP)
    second_hat = second_new / (1.0 - BETA_TWO**STEP)
    master_new = master - LEARN_RATE * (
        first_hat / (jnp.sqrt(second_hat) + ADAM_EPS) + WEIGHT_DECAY * master
    )
    return (weight_grad, master_new, first_new, second_new)


def shards(
    tokens,
    cotangent,
    segments,
    positions,
    qkv_weight,
    qkv_first,
    qkv_second,
    out_weight,
    out_first,
    out_second,
    in_weight,
    in_first,
    in_second,
    down_weight,
    down_first,
    down_second,
    norm_gains,
    gains_first,
    gains_second,
):
    devices = lax.axis_size("fsdp")
    rows = tokens.shape[0]
    seqs = rows // SEQ
    own_out, own_gain, own_down = out_weight.shape[0], norm_gains.shape[1], down_weight.shape[0]
    pack = own_out + 8
    down_pack = (own_down + 7) // 8 * 8

    qkv_low = lax.all_gather(qkv_weight.astype(BF), "fsdp", axis=0, tiled=True)
    gain_rows = jnp.pad(norm_gains, ((0, 6), (0, D - own_gain)))
    packed = jnp.concatenate([out_weight, gain_rows], axis=0).astype(BF)
    packed = lax.all_gather(packed, "fsdp", axis=0, tiled=True).reshape(devices, pack, D)
    out_low = packed[:, :own_out].reshape(D, D)
    gains = packed[:, own_out : own_out + 2, :own_gain].astype(F32)
    gains = gains.transpose(1, 0, 2).reshape(2, D)
    in_low = lax.all_gather(in_weight.astype(BF), "fsdp", axis=0, tiled=True)
    down_rows = jnp.pad(down_weight, ((0, down_pack - own_down), (0, 0))).astype(BF)
    down_low = lax.all_gather(down_rows, "fsdp", axis=0, tiled=True)
    down_low = down_low.reshape(devices, down_pack, D)[:, :own_down].reshape(FF, D)

    gain_one, gain_two = gains[0:1], gains[1:2]
    cosine, sine = rope_tables(positions)
    seg_col = segments.reshape(rows, 1)
    seg_row = segments.reshape(seqs, 1, SEQ)
    seg_row_spec = pl.BlockSpec((1, 1, SEQ), lambda i: (i, 0, 0))
    lse_spec = pl.BlockSpec((None, GROUPS * BLOCKS, 1, GROUP * BLK), lambda i: (i, 0, 0, 0))
    bias_scratch = pltpu.VMEM((BLOCKS, SPAN, BLK), F32)
    low_rows = shape_of((rows, D), BF)

    q, k, v, attended, lse, residual = run(
        attend_kernel,
        seqs,
        [rows_of(D), whole(1, D), whole(D, 3 * D), whole(D, D), rows_of(BLK), rows_of(BLK),
         rows_of(1), seg_row_spec],
        [rows_of(D)] * 4 + [lse_spec, rows_of(D)],
        [low_rows] * 4
        + [shape_of((seqs, GROUPS * BLOCKS, 1, GROUP * BLK), F32), shape_of((rows, D), F32)],
        [bias_scratch, pltpu.VMEM((SEQ, D), BF)],
        2 * rows * D * (4 * D) + 4 * rows * HEADS * SPAN * WIDE,
        rows * D * 14,
    )(tokens, gain_one, qkv_low, out_low, cosine, sine, seg_col, seg_row)

    activations, dres, gin, gdown, ggain_two = run(
        feed_kernel,
        seqs,
        [rows_of(D), rows_of(D), whole(1, D), whole(D, 2 * FF), whole(FF, D)],
        [rows_of(D), rows_of(D), kept(D, 2 * FF), kept(FF, D), kept(1, D)],
        [low_rows, shape_of((rows, D), F32), shape_of((D, 2 * FF), BF), shape_of((FF, D), BF),
         shape_of((1, D), F32)],
        [pltpu.VMEM((SEQ, D), BF), pltpu.VMEM((D, SEQ), BF), pltpu.VMEM((SEQ, D), F32),
         pltpu.VMEM((SEQ, D), F32), pltpu.VMEM((D, 2 * FF), F32), pltpu.VMEM((FF, D), F32)],
        2 * rows * D * FF * 9,
        rows * D * 12,
    )(residual, cotangent, gain_two, in_low, down_low)

    owned_in = lax.psum_scatter(gin, "fsdp", scatter_dimension=0, tiled=True)
    gdown = jnp.pad(
        gdown.reshape(devices, own_down, D), ((0, 0), (0, down_pack - own_down), (0, 0))
    ).reshape(devices * down_pack, D)
    owned_down = lax.psum_scatter(gdown, "fsdp", scatter_dimension=0, tiled=True)[:own_down]

    gmixed, gqkv, gout = run(
        attend_back_kernel,
        seqs,
        [rows_of(D), rows_of(D), whole(1, D), whole(D, D), rows_of(BLK), rows_of(BLK),
         rows_of(1), seg_row_spec, rows_of(D), rows_of(D), rows_of(D), rows_of(D), lse_spec],
        [rows_of(3 * D), kept(D, 3 * D), kept(D, D)],
        [shape_of((rows, 3 * D), BF), shape_of((D, 3 * D), BF), shape_of((D, D), BF)],
        [bias_scratch, pltpu.VMEM((D, SEQ), BF), pltpu.VMEM((SEQ, D), BF),
         pltpu.VMEM((SEQ, WIDE), F32), pltpu.VMEM((SEQ, WIDE), F32), pltpu.VMEM((SEQ, WIDE), F32),
         pltpu.VMEM((D, 3 * D), F32), pltpu.VMEM((D, D), F32)],
        2 * rows * D * (5 * D) + 10 * rows * HEADS * SPAN * WIDE,
        rows * D * 22,
    )(dres, tokens, gain_one, out_low, cosine, sine, seg_col, seg_row, q, k, v, attended, lse)

    owned_qkv = lax.psum_scatter(gqkv, "fsdp", scatter_dimension=0, tiled=True)

    input_grad, ggain_one = run(
        input_kernel,
        seqs,
        [rows_of(3 * D), rows_of(D), rows_of(D), whole(1, D), whole(D, 3 * D)],
        [rows_of(D), kept(1, D)],
        [shape_of((rows, D), F32), shape_of((1, D), F32)],
        [],
        2 * rows * D * 3 * D,
        rows * D * 16,
    )(gmixed, tokens, dres, gain_one, qkv_low)

    ggain = jnp.concatenate([ggain_one, ggain_two], axis=0)
    ggain = ggain.reshape(2, devices, own_gain).transpose(1, 0, 2).astype(BF)
    ggain = jnp.pad(ggain, ((0, 0), (0, 6), (0, D - own_gain)))
    packed = jnp.concatenate([gout.reshape(devices, own_out, D), ggain], axis=1)
    packed = packed.reshape(devices * pack, D)
    owned_pack = lax.psum_scatter(packed, "fsdp", scatter_dimension=0, tiled=True)
    owned_out = owned_pack[:own_out].astype(F32)
    owned_gain = owned_pack[own_out : own_out + 2, :own_gain].astype(F32)

    qkv_state = adam_step(qkv_weight, owned_qkv.astype(F32), qkv_first, qkv_second)
    out_state = adam_step(out_weight, owned_out, out_first, out_second)
    in_state = adam_step(in_weight, owned_in.astype(F32), in_first, in_second)
    down_state = adam_step(down_weight, owned_down.astype(F32), down_first, down_second)
    gains_state = adam_step(norm_gains, owned_gain, gains_first, gains_second)
    gains_delta = gains_state[1] - norm_gains
    return (
        activations,
        input_grad,
        *qkv_state,
        *out_state,
        *in_state,
        *down_state,
        gains_state[0],
        gains_delta,
        gains_state[2],
        gains_state[3],
    )


def solution(mesh):
    return jax.shard_map(
        shards,
        mesh=mesh,
        in_specs=(
            P("fsdp", None),
            P("fsdp", None),
            P("fsdp"),
            P("fsdp"),
            P("fsdp", None),
            P("fsdp", None),
            P("fsdp", None),
            P("fsdp", None),
            P("fsdp", None),
            P("fsdp", None),
            P("fsdp", None),
            P("fsdp", None),
            P("fsdp", None),
            P("fsdp", None),
            P("fsdp", None),
            P("fsdp", None),
            P(None, "fsdp"),
            P(None, "fsdp"),
            P(None, "fsdp"),
        ),
        out_specs=(
            P("fsdp", None),
            P("fsdp", None),
            P("fsdp", None),
            P("fsdp", None),
            P("fsdp", None),
            P("fsdp", None),
            P("fsdp", None),
            P("fsdp", None),
            P("fsdp", None),
            P("fsdp", None),
            P("fsdp", None),
            P("fsdp", None),
            P("fsdp", None),
            P("fsdp", None),
            P("fsdp", None),
            P("fsdp", None),
            P("fsdp", None),
            P("fsdp", None),
            P(None, "fsdp"),
            P(None, "fsdp"),
            P(None, "fsdp"),
            P(None, "fsdp"),
        ),
        check_vma=False,
    )
```

time: 1530 us -> 795 us (0.52); the launches traced: 1510 us -> 794 us
  local copies, waits for them, and re-layouts: 834 us -> 15.1 us
  waiting for transfers between devices: 57.2 us -> 585 us
  matrix products: 287 us -> 0 us
  blocking collectives: 171 us -> 0 us
  Pallas kernels: 0 us -> 155 us
  other arithmetic: 139 us -> 24.6 us
    reduce_scatter x3 -> x4, waiting for transfers between devices: 0.01 us -> 401 us  [the longest x1 106 us: shards(): owned_qkv = lax.psum_scatter(gqkv, 'fsdp', scatter_dimension=0, tiled=True)]
    dot_general x40 -> x0, matrix products: 287 us -> none  [the longest x8 42.9 us: block_scores(): jnp.einsum('bqhe,bkhe->bhqk', query_blocks, key_wide, preferred_element_t...]
    dynamic_update_slice x16 -> x0, local copies, waits for them, and re-layouts: 265 us -> none  [the longest x12 257 us: shards(): lax.map(attend_back, (seq_queries, seq_keys, seq_values, seq_grad_heads,...]
    slice x118 -> x5, local copies, waits for them, and re-layouts: 224 us -> 4.64 us  [the longest x1 2.45 us: shards(): out_low = packed[:, :own_out].reshape(D, D)]
    pallas_call x0 -> x4, Pallas kernels: none -> 155 us  [the longest x1 51.8 us: shards(): run(attend_back_kernel, seqs, [rows_of(D), rows_of(D), whole(1, D), whole...]
    unnamed x2 -> x0, blocking collectives: 128 us -> none
    all_gather x4, waiting for transfers between devices: 57.1 us -> 183 us  [the longest x1 58.7 us: shards(): qkv_low = lax.all_gather(qkv_weight.astype(BF), 'fsdp', axis=0, tiled=True)]
    reshape x51 -> x3, local copies, waits for them, and re-layouts: 131 us -> 8.15 us  [the longest x1 3.67 us: shards(): down_low.reshape(devices, down_pack, D)[:, :own_down].reshape(FF, D)]
  transfers between devices with their start and end apart: 11 -> 8, of which waited for: 1 -> 8; matrix products, arithmetic and copies ran while one was open for 82% -> 4% of each run, Pallas kernels for 0% -> 5%
where the time goes in v1:
time: 795 us; the launch traced here: 794 us
  waiting for transfers between devices  585 us (74%)
  Pallas kernels  155 us (19%)
  other arithmetic  24.6 us (3%)
  local copies, waits for them, and re-layouts  15.1 us (2%)
  between operations  14.4 us (2%)
    reduce_scatter x1, waiting for transfers between devices, shards(): owned_qkv = lax.psum_scatter(gqkv, 'fsdp', scatter_dimension=0, tiled=True)  106 us
    reduce_scatter x1, waiting for transfers between devices, shards(): owned_in = lax.psum_scatter(gin, 'fsdp', scatter_dimension=0, tiled=True)  106 us
    reduce_scatter x1, waiting for transfers between devices, shards(): lax.psum_scatter(gdown, 'fsdp', scatter_dimension=0, tiled=True)[:own_down]  99.4 us
    reduce_scatter x1, waiting for transfers between devices, shards(): lax.psum_scatter(packed, 'fsdp', scatter_dimension=0, tiled=True)  90.5 us
    all_gather x1, waiting for transfers between devices, shards(): qkv_low = lax.all_gather(qkv_weight.astype(BF), 'fsdp', axis=0, tiled=True)  58.7 us
    all_gather x1, waiting for transfers between devices, shards(): down_low = lax.all_gather(down_rows, 'fsdp', axis=0, tiled=True)  53.8 us
    pallas_call x1, Pallas kernels, shards(): run(attend_back_kernel, seqs, [rows_of(D), rows_of(D), whole(1, D), whole...  51.8 us
    pallas_call x1, Pallas kernels, shards(): run(feed_kernel, seqs, [rows_of(D), rows_of(D), whole(1, D), whole(D, 2 *...  50 us
  transfers between devices with their start and end apart: 8, of which 8 were waited for; matrix products, arithmetic and copies ran while one was open for 4% of the time, Pallas kernels for 5%

profile of v1, /device:TPU:0, one launch (start us, length us, event | category | flops | bytes accessed | tf_op | source)
XLA Modules:
  0.0 794.3 jit_solution(7046121945960930563)
XLA Ops:
  7.2 0.0 all-gather.5.cloned.1.call-start
  7.2 0.7 convert.20
  7.9 0.9 convert.19
  8.8 0.6 fusion.8
  9.4 0.0 all-gather.5.cloned.1.call-update
  9.5 0.0 all-gather.11.cloned.1.call-start
  9.5 0.9 convert.21
  10.4 0.6 pad.19
  11.1 0.0 all-gather.11.cloned.1.call-update
  11.1 0.0 all-gather.7.cloned.1.call-start
  11.1 1.6 convert_element_type.49
  12.7 0.0 all-gather.7.cloned.1.call-update
  12.7 0.0 all-gather.9.cloned.1.call-start
  12.8 1.6 convert_element_type.52
  14.4 0.0 all-gather.9.cloned.1.call-update
  14.4 0.0 reduce-scatter.7.cloned.1.call-start
  14.5 0.7 convert_element_type.50
  15.2 2.1 copy.53.segc_ref
  17.2 3.7 fusion.2
  21.0 3.0 pad_maximum_fusion
  24.0 45.2 %all-gather.5.cloned.1.call-done = bf16[1024,768]{1,0:T(8,128)(2,1)} async-done(((bf16[32,768]{1,0:T(8,128)(2,1)}), bf16[1024,768]{1,0:T(8,128)(2,1)}) %all-gather.5.cloned.1.call-update) | async-done | bytes 1572880 | tf_op jit(solution)/shard_map/all_gather | solution.py:357
  69.1 0.8 slice.40
  70.0 2.4 slice.42
  72.5 0.7 slice.35.gain_ref
  73.1 0.7 slice.32.gain_ref
  73.8 53.8 %all-gather.11.cloned.1.call-done = bf16[1280,768]{1,0:T(8,128)(2,1)} async-done(((bf16[40,768]{1,0:T(8,128)(2,1)}), bf16[1280,768]{1,0:T(8,128)(2,1)}) %all-gather.11.cloned.1.call-update) | async-done | bytes 1966096 | tf_op jit(solution)/shard_map/all_gather | solution.py:363
  127.6 3.7 reshape.92.wd_ref
  131.3 58.7 %all-gather.7.cloned.1.call-done.wqkv_ref = bf16[768,2304]{1,0:T(8,128)(2,1)} async-done(((bf16[24,2304]{1,0:T(8,128)(2,1)}), bf16[768,2304]{1,0:T(8,128)(2,1)}) %all-gather.7.cloned.1.call-update) | async-done | bytes 3538960 | tf_op jit(solution)/shard_map/all_gather | solution.py:354
  190.0 37.4 %shard_map.354 = (bf16[2048,768]{1,0:T(8,128)(2,1)}, bf16[2048,768]{1,0:T(8,128)(2,1)}, bf16[2048,768]{1,0:T(8,128)(2,1)}, bf16[2048,768]{1,0:T(8,128)(2,1)}, f3...) custom-call(bf16[2048,768]{1,0:T(8,128)(2,1)} %tok_ref.5, f32[1,768]{1,0:T(1,128)} %slice.32.gain_ref, ...), custom_call_target="tpu_custom_call" | custom-call | flops 16106127360 | bytes 22020096 | tf_op jit(solution)/shard_map/pallas_call | solution.py:375
  227.5 24.8 %all-gather.9.cloned.1.call-done.wi_ref = bf16[768,2304]{1,0:T(8,128)(2,1)} async-done(((bf16[24,2304]{1,0:T(8,128)(2,1)}), bf16[768,2304]{1,0:T(8,128)(2,1)}) %all-gather.9.cloned.1.call-update) | async-done | bytes 3538960 | tf_op jit(solution)/shard_map/all_gather | solution.py:361
  252.3 50.0 %shard_map.355 = (bf16[2048,768]{1,0:T(8,128)(2,1)}, f32[2048,768]{1,0:T(8,128)}, bf16[768,2304]{1,0:T(8,128)(2,1)}, bf16[1152,768]{1,0:T(8,128)(2,1)}, f32[1,768]{1,0:T(1,128)}) custom-call(f32[2048,768]{1,0:T(8,128)} %get-tuple-element.38.res_ref, bf16[2048,768]{1,0:T(8,128)(2,1)} %cot_ref.1, f32[1,768]{1,0:T(1,128)} %slice.35.gain_ref, ...), custom_call_target="tpu_custom_call" | custom-call | flops 32614907904 | bytes 18874368 | tf_op jit(solution)/shard_map/pallas_call | solution.py:388
  302.3 0.7 convert.23
  303.0 51.8 %shard_map.356 = (bf16[2048,2304]{1,0:T(8,128)(2,1)}, bf16[768,2304]{1,0:T(8,128)(2,1)}, bf16[768,768]{1,0:T(8,128)(2,1)}) custom-call(f32[2048,768]{1,0:T(8,128)} %get-tuple-element.40.dres_ref, bf16[2048,768]{1,0:T(8,128)(2,1)} %tok_ref.5, f32[1,768]{1,0:T(1,128)} %slice.32.gain_ref, bf16[768,768]{1,0:T(8,128)(2,1)} %bitcast.16, ...), custom_call_target="tpu_custom_call" | custom-call | flops 28185722880 | bytes 34603008 | tf_op jit(solution)/shard_map/pallas_call | solution.py:407
  354.8 15.6 %shard_map.357 = (f32[2048,768]{1,0:T(8,128)}, f32[1,768]{1,0:T(1,128)}) custom-call(bf16[2048,2304]{1,0:T(8,128)(2,1)} %get-tuple-element.46.gm_ref, bf16[2048,768]{1,0:T(8,128)(2,1)} %tok_ref.5, f32[2048,768]{1,0:T(8,128)} %get-tuple-element.40.dres_ref, f32[1,768]{1,0:T(1,128)} %slice.32.gain_ref, bf16[768,2304]{1,0:T(8,128)(2,1)} %all-gather.7.cloned.1.call-done.wqkv_ref), custom_call_target="tpu_custom_call" | custom-call | flops 7247757312 | bytes 25165824 | tf_op jit(solution)/shard_map/pallas_call | solution.py:423
  370.4 0.7 convert.22
  371.1 0.1 convert_element_type.54
  371.3 1.4 fusion.1
  372.6 0.0 reduce-scatter.7.cloned.1.call-update
  372.7 0.0 reduce-scatter.11.cloned.1.call-start
  372.7 2.4 reshape.95
  375.1 1.4 pad.21
  376.6 0.0 reduce-scatter.11.cloned.1.call-update
  376.6 0.0 reduce-scatter.5.cloned.1.call-start
  376.6 0.0 copy-start.13
  376.7 0.0 copy-start.14
  376.7 0.0 copy-start.11
  376.7 0.0 copy-start.12
  376.7 0.0 copy-start.9
  376.7 0.0 copy-start.10
  376.7 0.6 reduce-scatter.5.cloned.1.call-update
  377.3 0.0 copy-start.1
  377.4 0.0 copy-start.5
  377.4 0.0 reduce-scatter.9.cloned.1.call-start
  377.4 0.0 copy-start.7
  377.5 0.7 reduce-scatter.9.cloned.1.call-update
  378.1 90.5 %reduce-scatter.7.cloned.1.call-done = bf16[32,768]{1,0:T(8,128)(2,1)} async-done(((bf16[1024,768]{1,0:T(8,128)(2,1)}), bf16[32,768]{1,0:T(8,128)(2,1)}) %reduce-scatter.7.cloned.1.call-update) | async-done | bytes 49168 | tf_op jit(solution)/shard_map/reduce_scatter | solution.py:439
  468.7 1.3 subtract_subtract_fusion
  469.9 1.5 multiply_subtract_fusion.3
  471.4 99.4 %reduce-scatter.11.cloned.1.call-done = bf16[40,768]{1,0:T(8,128)(2,1)} async-done(((bf16[1280,768]{1,0:T(8,128)(2,1)}), bf16[40,768]{1,0:T(8,128)(2,1)}) %reduce-scatter.11.cloned.1.call-update) | async-done | bytes 61456 | tf_op jit(solution)/shard_map/reduce_scatter | solution.py:405
  570.8 1.6 multiply_subtract_fusion.2
  572.4 105.8 %reduce-scatter.5.cloned.1.call-done = bf16[24,2304]{1,0:T(8,128)(2,1)} async-done(((bf16[768,2304]{1,0:T(8,128)(2,1)}), bf16[24,2304]{1,0:T(8,128)(2,1)}) %reduce-scatter.5.cloned.1.call-update) | async-done | bytes 110608 | tf_op jit(solution)/shard_map/reduce_scatter | solution.py:421
  678.3 1.9 multiply_subtract_fusion.1
  680.1 105.5 %reduce-scatter.9.cloned.1.call-done = bf16[24,2304]{1,0:T(8,128)(2,1)} async-done(((bf16[768,2304]{1,0:T(8,128)(2,1)}), bf16[24,2304]{1,0:T(8,128)(2,1)}) %reduce-scatter.9.cloned.1.call-update) | async-done | bytes 110608 | tf_op jit(solution)/shard_map/reduce_scatter | solution.py:401
  785.6 1.8 multiply_subtract_fusion
  (28 shorter events, 0.1 us)
Async XLA Ops:
  7.2 62.0 %all-gather.5.cloned.1.call-start = ((), (), s32[]{:S(2)}) async-start(), calls=%async_computation.4 | async-start | bytes 1622016 | tf_op jit(solution)/shard_map/all_gather | solution.py:357
  9.5 118.2 %all-gather.11.cloned.1.call-start = ((), (), s32[]{:S(2)}) async-start(), calls=%async_computation.7 | async-start | bytes 2027520 | tf_op jit(solution)/shard_map/all_gather | solution.py:363
  11.1 179.0 %all-gather.7.cloned.1.call-start = ((), (), s32[]{:S(2)}) async-start(), calls=%async_computation.5 | async-start | bytes 3649536 | tf_op jit(solution)/shard_map/all_gather | solution.py:354
  12.7 239.5 %all-gather.9.cloned.1.call-start = ((), (), s32[]{:S(2)}) async-start(), calls=%async_computation.6 | async-start | bytes 3649536 | tf_op jit(solution)/shard_map/all_gather | solution.py:361
  14.4 454.2 %reduce-scatter.7.cloned.1.call-start = ((), (), s32[]{:S(2)}) async-start(), calls=%async_computation.9 | async-start | bytes 1622016 | tf_op jit(solution)/shard_map/reduce_scatter | solution.py:439
  354.8 16.4 %copy-start = (bf16[768,768]{1,0:T(8,128)(2,1)S(1)}, bf16[768,768]{1,0:T(8,128)(2,1)}, u32[]{:S(2)}) copy-start(bf16[768,768]{1,0:T(8,128)(2,1)} %get-tuple-element.49) | copy-start | bytes 3538948
  372.7 198.1 %reduce-scatter.11.cloned.1.call-start = ((), (), s32[]{:S(2)}) async-start(), calls=%async_computation.11 | async-start | bytes 2027520 | tf_op jit(solution)/shard_map/reduce_scatter | solution.py:405
  376.6 301.7 %reduce-scatter.5.cloned.1.call-start = ((), (), s32[]{:S(2)}) async-start(), calls=%async_computation.8 | async-start | bytes 3649536 | tf_op jit(solution)/shard_map/reduce_scatter | solution.py:421
  376.6 92.0 %copy-start.13 = (f32[2,24]{1,0:T(2,128)S(1)}, f32[2,24]{1,0:T(2,128)}, u32[]{:S(2)}) copy-start(f32[2,24]{1,0:T(2,128)} %param.35) | copy-start | bytes 580
  376.7 92.0 %copy-start.14 = (f32[2,24]{1,0:T(2,128)S(1)}, f32[2,24]{1,0:T(2,128)}, u32[]{:S(2)}) copy-start(f32[2,24]{1,0:T(2,128)} %param.36) | copy-start | bytes 580
  376.7 92.0 %copy-start.15 = (f32[2,24]{1,0:T(2,128)S(1)}, f32[2,24]{1,0:T(2,128)}, u32[]{:S(2)}) copy-start(f32[2,24]{1,0:T(2,128)} %param.37) | copy-start | bytes 580
  376.7 93.3 %copy-start.4 = (f32[24,768]{1,0:T(8,128)S(1)}, f32[24,768]{1,0:T(8,128)}, u32[]{:S(2)}) copy-start(f32[24,768]{1,0:T(8,128)} %param.26) | copy-start | bytes 221188
  376.7 93.2 %copy-start.11 = (f32[24,768]{1,0:T(8,128)S(1)}, f32[24,768]{1,0:T(8,128)}, u32[]{:S(2)}) copy-start(f32[24,768]{1,0:T(8,128)} %param.27) | copy-start | bytes 221188
  376.7 93.2 %copy-start.12 = (f32[24,768]{1,0:T(8,128)S(1)}, f32[24,768]{1,0:T(8,128)}, u32[]{:S(2)}) copy-start(f32[24,768]{1,0:T(8,128)} %param.28) | copy-start | bytes 221188
  376.7 194.1 %copy-start.3 = (f32[36,768]{1,0:T(8,128)S(1)}, f32[36,768]{1,0:T(8,128)}, u32[]{:S(2)}) copy-start(f32[36,768]{1,0:T(8,128)} %param.32) | copy-start | bytes 331780
  376.7 194.1 %copy-start.9 = (f32[36,768]{1,0:T(8,128)S(1)}, f32[36,768]{1,0:T(8,128)}, u32[]{:S(2)}) copy-start(f32[36,768]{1,0:T(8,128)} %param.33) | copy-start | bytes 331780
  376.7 194.1 %copy-start.10 = (f32[36,768]{1,0:T(8,128)S(1)}, f32[36,768]{1,0:T(8,128)}, u32[]{:S(2)}) copy-start(f32[36,768]{1,0:T(8,128)} %param.34) | copy-start | bytes 331780
  377.3 300.9 %copy-start.1 = (f32[24,2304]{1,0:T(8,128)S(1)}, f32[24,2304]{1,0:T(8,128)}, u32[]{:S(2)}) copy-start(f32[24,2304]{1,0:T(8,128)} %param.23) | copy-start | bytes 663556
  377.4 300.9 %copy-start.5 = (f32[24,2304]{1,0:T(8,128)S(1)}, f32[24,2304]{1,0:T(8,128)}, u32[]{:S(2)}) copy-start(f32[24,2304]{1,0:T(8,128)} %param.24) | copy-start | bytes 663556
  377.4 300.9 %copy-start.6 = (f32[24,2304]{1,0:T(8,128)S(1)}, f32[24,2304]{1,0:T(8,128)}, u32[]{:S(2)}) copy-start(f32[24,2304]{1,0:T(8,128)} %param.25) | copy-start | bytes 663556
  377.4 408.3 %reduce-scatter.9.cloned.1.call-start = ((), (), s32[]{:S(2)}) async-start(), calls=%async_computation.10 | async-start | bytes 3649536 | tf_op jit(solution)/shard_map/reduce_scatter | solution.py:401
  377.4 408.2 %copy-start.2 = (f32[24,2304]{1,0:T(8,128)S(1)}, f32[24,2304]{1,0:T(8,128)}, u32[]{:S(2)}) copy-start(f32[24,2304]{1,0:T(8,128)} %param.29) | copy-start | bytes 663556
  377.4 408.2 %copy-start.7 = (f32[24,2304]{1,0:T(8,128)S(1)}, f32[24,2304]{1,0:T(8,128)}, u32[]{:S(2)}) copy-start(f32[24,2304]{1,0:T(8,128)} %param.30) | copy-start | bytes 663556
  377.5 408.2 %copy-start.8 = (f32[24,2304]{1,0:T(8,128)S(1)}, f32[24,2304]{1,0:T(8,128)}, u32[]{:S(2)}) copy-start(f32[24,2304]{1,0:T(8,128)} %param.31) | copy-start | bytes 663556
Sparse Core Ops, SparseCore 0:
  11.5 57.6 all-gather.4
  72.6 54.9 all-gather.10
  131.1 58.8 all-gather.6
  193.4 58.8 all-gather.8
  372.8 95.8 reduce-scatter.6
  473.8 96.9 reduce-scatter.10
  576.2 102.0 reduce-scatter.4
  683.7 101.8 reduce-scatter.8
